TPU v7x, 32 devices: a whole 2x2x4 slice. The times are simulated.
32 devices in a mesh: groups: 2 (over y), row: 16 (over z, x, core).
Axes of the slice: x: 2, y: 2, z: 4, core: 2. Of those that a mesh axis runs over, the one named last changes fastest.
Arguments:
- pair: bfloat16 [32, 128, 128, 128], P(('groups', 'row')), parts along dimension 0, may hold values from -6 to 6
- comp_len: int32 [4], P('groups'), parts along dimension 0, may hold values from 129 to 384, as said below
- tile_place: int32 [32], P('groups'), parts along dimension 0, may hold values from 0 to 15, each once
- in_gain: float32 [128], replicated, may hold values from 0.1 to 1.9
- in_bias: float32 [128], replicated, may hold values from -2 to 2
- proj_weight: bfloat16 [128, 512], replicated, may hold values from -0.5 to 0.5
- gate_weight: bfloat16 [128, 128], replicated, may hold values from -0.5 to 0.5
- out_gain: float32 [128], replicated, may hold values from 0.1 to 1.9
- out_bias: float32 [128], replicated, may hold values from -2.5 to 2.5
- out_weight: bfloat16 [128, 128], replicated, may hold values from -0.5 to 0.5
Outputs:
- update: bfloat16 [32, 128, 128, 128], P(('groups', 'row')), parts along dimension 0
There are 2 independent parts, one for each index of `groups`. A program takes and returns all parts, laid end to end along the dimension named above; an argument that names none is the same for every part. Nothing has to cross between parts.
Inputs may be any that keep to these rules, and one draw needn't show every extreme that they name: `comp_len`: complex 0 holds exactly 384 tokens; complex 1 holds more than 128 tokens, and the tiles of both complexes together fit into 16 slots. `tile_place`: A permutation of the 16 slots.
All inputs are finite; a program needn't handle non-finite values.
Results may differ from a plain program's by a relative error of at most 0.0061.
Values may be sent and summed in bfloat16 or wider, within the bound.
A program may use at most 128 MiB of HBM per device.

v0:
```python
import jax
import jax.numpy as jnp
from jax import lax
from jax.sharding import PartitionSpec as P


def pick_slot(onehot, values):
    return jnp.sum(jnp.where(onehot, values[None, :], 0), 1)


def tile_tables(comp_len, tile_place, tiles, tile_side, most_tiles):
    counts = (comp_len + tile_side - 1) // tile_side
    areas = counts * counts
    starts = jnp.cumsum(areas) - areas
    numbers = jnp.arange(tiles, dtype=jnp.int32)
    inside = (
        (numbers[:, None] >= starts[None, :]) & (numbers[:, None] < (starts + areas)[None, :])
    ).astype(jnp.int32)
    used = jnp.sum(inside, 1)
    sides = jnp.sum(inside * counts[None, :], 1)
    firsts = jnp.sum(inside * starts[None, :], 1)
    lengths = jnp.sum(inside * comp_len[None, :], 1)
    local_number = numbers - firsts
    safe_side = jnp.maximum(sides, 1)
    tile_row = local_number // safe_side
    tile_col = local_number % safe_side
    onehot = tile_place[None, :] == numbers[:, None]
    slot_used = pick_slot(onehot, used)
    slot_side = pick_slot(onehot, sides)
    slot_first = pick_slot(onehot, firsts)
    slot_length = pick_slot(onehot, lengths)
    slot_row = pick_slot(onehot, tile_row)
    slot_col = pick_slot(onehot, tile_col)
    steps_k = jnp.arange(most_tiles, dtype=jnp.int32)
    left_number = jnp.clip(
        slot_first[:, None] + slot_row[:, None] * slot_side[:, None] + steps_k[None, :],
        0,
        tiles - 1,
    )
    right_number = jnp.clip(
        slot_first[:, None] + slot_col[:, None] * slot_side[:, None] + steps_k[None, :],
        0,
        tiles - 1,
    )
    left_slot = jnp.sum(
        jnp.where(left_number[:, :, None] == numbers[None, None, :], tile_place[None, None, :], 0),
        2,
    )
    right_slot = jnp.sum(
        jnp.where(right_number[:, :, None] == numbers[None, None, :], tile_place[None, None, :], 0),
        2,
    )
    valid = ((steps_k[None, :] < slot_side[:, None]) & (slot_used[:, None] > 0)).astype(jnp.float32)
    tokens = jnp.arange(tile_side, dtype=jnp.int32)
    row_ok = (
        (slot_row[:, None] * tile_side + tokens[None, :] < slot_length[:, None])
        & (slot_used[:, None] > 0)
    ).astype(jnp.float32)
    col_ok = (
        (slot_col[:, None] * tile_side + tokens[None, :] < slot_length[:, None])
        & (slot_used[:, None] > 0)
    ).astype(jnp.float32)
    return (left_slot, right_slot, valid, row_ok, col_ok)


def shards(
    pair,
    comp_len,
    tile_place,
    in_gain,
    in_bias,
    proj_weight,
    gate_weight,
    out_gain,
    out_bias,
    out_weight,
):
    tiles = tile_place.shape[0]
    tile_side = pair.shape[1]
    pair_width = pair.shape[3]
    channels = out_weight.shape[0]
    devices_row = lax.axis_size("row")
    group_size = channels // devices_row
    most_tiles = 2 + tiles // 16
    block_rows = 16
    left_slot, right_slot, valid, row_ok, col_ok = tile_tables(
        comp_len, tile_place, tiles, tile_side, most_tiles
    )
    own_slot = lax.axis_index("row")
    rows_live = lax.dynamic_index_in_dim(row_ok, own_slot, 0, keepdims=False)
    cols_live = lax.dynamic_index_in_dim(col_ok, own_slot, 0, keepdims=False)
    pair_mask = (rows_live[:, None] * cols_live[None, :]).reshape(1, tile_side * tile_side)
    flattened = pair.reshape(tile_side * tile_side, pair_width).astype(jnp.float32)
    average = jnp.mean(flattened, 1, keepdims=True)
    centred = flattened - average
    variance = jnp.mean(centred * centred, 1, keepdims=True)
    normed = (centred * lax.rsqrt(variance + 1e-05) * in_gain + in_bias).astype(jnp.bfloat16)
    gating = jax.nn.sigmoid(jnp.dot(normed, gate_weight, preferred_element_type=jnp.float32))

    def operand(which):
        weights = proj_weight[:, 2 * which * channels : (2 * which + 2) * channels]
        projected = lax.dot_general(
            weights, normed, (((0,), (1,)), ((), ())), preferred_element_type=jnp.float32
        )
        result = pair_mask * jax.nn.sigmoid(projected[:channels]) * projected[channels:]
        return result.astype(jnp.bfloat16).reshape(devices_row, group_size, 1, tile_side, tile_side)

    left_tiles = operand(0)
    right_tiles = operand(1)
    left_group = lax.all_to_all(left_tiles, "row", split_axis=0, concat_axis=2, tiled=True)[0]
    right_group = lax.all_to_all(right_tiles, "row", split_axis=0, concat_axis=2, tiled=True)[0]
    group_width = left_group.shape[0]
    initial = jnp.zeros((group_width, tiles, tile_side, tile_side), jnp.bfloat16)

    def one_block(block_index, totals):
        first_row = block_index * block_rows
        left_list = lax.dynamic_slice_in_dim(left_slot, first_row, block_rows, 0).reshape(-1)
        right_list = lax.dynamic_slice_in_dim(right_slot, first_row, block_rows, 0).reshape(-1)
        weights = lax.dynamic_slice_in_dim(valid, first_row, block_rows, 0).astype(jnp.bfloat16)
        picked_left = jnp.take(left_group, left_list, axis=1).reshape(
            group_width, block_rows, most_tiles, tile_side, tile_side
        )
        picked_left = picked_left * weights[None, :, :, None, None]
        picked_right = jnp.take(right_group, right_list, axis=1).reshape(
            group_width, block_rows, most_tiles, tile_side, tile_side
        )
        products = jnp.einsum(
            "gtkia,gtkja->gtij", picked_left, picked_right, preferred_element_type=jnp.float32
        )
        return lax.dynamic_update_slice_in_dim(totals, products.astype(jnp.bfloat16), first_row, 1)

    mixed = lax.fori_loop(0, tiles // block_rows, one_block, initial)[None]
    mixed = mixed.reshape(group_size, tiles, tile_side, tile_side)
    returned = lax.all_to_all(mixed, "row", split_axis=1, concat_axis=0, tiled=True)
    gathered = returned.reshape(channels, tile_side * tile_side).astype(jnp.float32)
    mixed_mean = jnp.mean(gathered, 0, keepdims=True)
    mixed_centred = gathered - mixed_mean
    mixed_variance = jnp.mean(mixed_centred * mixed_centred, 0, keepdims=True)
    mixed_norm = (
        mixed_centred * lax.rsqrt(mixed_variance + 1e-05) * out_gain[:, None] + out_bias[:, None]
    ).astype(jnp.bfloat16)
    projected_out = lax.dot_general(
        mixed_norm, out_weight, (((0,), (0,)), ((), ())), preferred_element_type=jnp.float32
    )
    return (
        (gating * projected_out).astype(jnp.bfloat16).reshape(1, tile_side, tile_side, pair_width)
    )


def solution(mesh):
    placed = (
        P(("groups", "row"), None, None, None),
        P("groups"),
        P("groups"),
        P(),
        P(),
        P(),
        P(),
        P(),
        P(),
        P(),
    )
    return jax.shard_map(
        shards,
        mesh=mesh,
        in_specs=placed,
        out_specs=P(("groups", "row"), None, None, None),
        check_vma=False,
    )
```

profile of v0, /device:TPU:15, one launch (start us, length us, event | category | flops | bytes accessed | tf_op | source)
XLA Modules:
  0.0 414.8 jit_solution(10548372518538345003)
XLA Ops:
  0.0 3.5 convert_reduce_fusion
  3.6 6.0 %multiply_reduce_fusion = f32[128,128]{1,0:T(8,128)S(1)} fusion(bf16[1,128,128,128]{3,2,1,0:T(8,128)(2,1)} %param.12, f32[128,128]{1,0:T(8,128)S(1)} %get-tuple-element.49), kind=kLoop, calls=%fused_computation.46 | loop fusion | flops 8372224 | bytes 4325376 | tf_op jit(solution)/shard_map/reduce_sum | solution.py:96
  9.6 5.0 %fusion.27 = bf16[16384,128]{1,0:T(8,128)(2,1)S(1)} fusion(bf16[1,128,128,128]{3,2,1,0:T(8,128)(2,1)S(1)} %copy-done.2, f32[128]{0:T(128)S(1)} %copy-done.6, f32[128]{0:T(128)S(1)} %copy-done.7, f32[16384]{0:T(1024)S(1)} %rsqrt_bitcast_fusion.1, f32[16384]{0:T(1024)S(1)} %get-tuple-element.48), kind=kLoop, calls=%fused_computation.45 | loop fusion | flops 12582912 | bytes 8520704 | tf_op jit(solution)/shard_map/convert_element_type | solution.py:97
  14.6 8.0 %convolution_bitcast_fusion = f32[256,16384]{0,1:T(8,128)} fusion(bf16[16384,128]{1,0:T(8,128)(2,1)S(1)} %fusion.27, bf16[128,512]{1,0:T(8,128)(2,1)S(1)} %copy-done.3), kind=kOutput, calls=%fused_computation.2 | convolution fusion | flops 1073741824 | bytes 21037056 | tf_op jit(solution)/shard_map/dot_general | solution.py:102
  22.7 8.0 %convolution_bitcast_fusion.1 = f32[256,16384]{0,1:T(8,128)} fusion(bf16[16384,128]{1,0:T(8,128)(2,1)S(1)} %fusion.27, bf16[128,512]{1,0:T(8,128)(2,1)S(1)} %copy-done.3), kind=kOutput, calls=%fused_computation.3 | convolution fusion | flops 1073741824 | bytes 21037056 | tf_op jit(solution)/shard_map/dot_general | solution.py:102
  36.6 15.0 %fusion.19 = (bf16[128,16384]{0,1:T(8,128)(2,1)}, bf16[128,16384]{0,1:T(8,128)(2,1)}) fusion(f32[256,16384]{0,1:T(8,128)} %convolution_bitcast_fusion.1, f32[16384]{0:T(1024)S(1)} %multiply_bitcast_fusion, f32[256,16384]{0,1:T(8,128)} %convolution_bitcast_fusion), kind=kLoop, calls=%fused_computation.34 | loop fusion | flops 25165824 | bytes 42008576 | tf_op jit(solution)/shard_map/convert_element_type | solution.py:106
  51.6 6.4 %copy.26 = bf16[128,16384]{1,0:T(8,128)(2,1)} copy(bf16[128,16384]{0,1:T(8,128)(2,1)} %get-tuple-element.46) | data formatting | bytes 8388608 | tf_op jit(solution)/shard_map/convert_element_type | solution.py:106
  58.1 5.4 %copy.51 = bf16[16,8,128,128]{3,2,1,0:T(8,128)(2,1)} copy(bf16[16,8,128,128]{3,1,2,0:T(8,128)(2,1)} %bitcast.107) | data formatting | bytes 8388608
  63.4 6.6 %all-to-all-start = ((bf16[16,8,1,128,128]{4,3,1,2,0:T(8,128)(2,1)}), bf16[16,8,1,128,128]{4,3,1,2,0:T(8,128)(2,1)}, u32[]{:S(2)}, u32[]{:S(2)}) async-start(bf16[16,8,1,128,128]{4,3,1,2,0:T(8,128)(2,1)} %bitcast.106), calls=%async_computation | async-start | bytes 8388608 | tf_op jit(solution)/shard_map/all_to_all | solution.py:110
  70.0 6.4 %copy.30 = bf16[128,16384]{1,0:T(8,128)(2,1)} copy(bf16[128,16384]{0,1:T(8,128)(2,1)} %get-tuple-element.47) | data formatting | bytes 8388608 | tf_op jit(solution)/shard_map/convert_element_type | solution.py:106
  76.4 5.4 %copy.50 = bf16[16,8,128,128]{3,2,1,0:T(8,128)(2,1)} copy(bf16[16,8,128,128]{3,1,2,0:T(8,128)(2,1)} %bitcast.108) | data formatting | bytes 8388608
  81.7 80.7 %all-to-all-done = bf16[16,8,1,128,128]{4,3,1,2,0:T(8,128)(2,1)} async-done(((bf16[16,8,1,128,128]{4,3,1,2,0:T(8,128)(2,1)}), bf16[16,8,1,128,128]{4,3,1,2,0:T(8,128)(2,1)}, u32[]{:S(2)}, u32[]{:S(2)}) %all-to-all-start) | async-done | bytes 4194336 | tf_op jit(solution)/shard_map/all_to_all | solution.py:110
  162.5 4.9 %all-to-all-start.1 = ((bf16[16,8,1,128,128]{4,3,1,2,0:T(8,128)(2,1)}), bf16[16,8,1,128,128]{4,3,1,2,0:T(8,128)(2,1)}, u32[]{:S(2)}, u32[]{:S(2)}) async-start(bf16[16,8,1,128,128]{4,3,1,2,0:T(8,128)(2,1)} %bitcast.105), calls=%async_computation.1 | async-start | bytes 8388608 | tf_op jit(solution)/shard_map/all_to_all | solution.py:111
  168.1 8.5 %gather_fusion = bf16[48,8,128,128]{3,2,1,0:T(8,128)(2,1)} fusion(bf16[8,16,128,128]{3,2,0,1:T(8,128)(2,1)} %bitcast.12, s32[1024]{0:T(1024)S(1)} %pad_clamp_fusion.1), kind=kCustom, calls=%fused_computation.clone | custom fusion | bytes 25166016 | tf_op jit(solution)/shard_map/while/body/eval_jaxpr/jit(_take)/gather | solution.py:120
  176.6 10.7 %broadcast_select_fusion.1 = bf16[48,8,128,128]{3,2,1,0:T(8,128)(2,1)} fusion(bf16[48,8,128,128]{3,2,1,0:T(8,128)(2,1)} %gather_fusion, pred[48]{0:T(512)(128)(4,1)S(1)} %compare_and_fusion.1), kind=kLoop, calls=%fused_computation.14 | loop fusion | flops 6291456 | bytes 25165872 | tf_op jit(solution)/shard_map/while/body/eval_jaxpr/jit(_take)/select_n | solution.py:120
  187.3 72.5 %all-to-all-done.1 = bf16[16,8,1,128,128]{4,3,1,2,0:T(8,128)(2,1)} async-done(((bf16[16,8,1,128,128]{4,3,1,2,0:T(8,128)(2,1)}), bf16[16,8,1,128,128]{4,3,1,2,0:T(8,128)(2,1)}, u32[]{:S(2)}, u32[]{:S(2)}) %all-to-all-start.1) | async-done | bytes 4194336 | tf_op jit(solution)/shard_map/all_to_all | solution.py:111
  259.8 8.6 %gather_fusion.1 = bf16[48,8,128,128]{3,2,1,0:T(8,128)(2,1)} fusion(bf16[8,16,128,128]{3,2,0,1:T(8,128)(2,1)} %bitcast.19, s32[1024]{0:T(1024)S(1)} %pad_clamp_fusion), kind=kCustom, calls=%fused_computation.1.clone | custom fusion | bytes 25166016 | tf_op jit(solution)/shard_map/while/body/eval_jaxpr/jit(_take)/gather | solution.py:124
  268.4 10.8 %broadcast_select_fusion = bf16[48,8,128,128]{3,2,1,0:T(8,128)(2,1)} fusion(bf16[48,8,128,128]{3,2,1,0:T(8,128)(2,1)} %gather_fusion.1, pred[48]{0:T(512)(128)(4,1)S(1)} %compare_and_fusion), kind=kLoop, calls=%fused_computation.13 | loop fusion | flops 6291456 | bytes 25165872 | tf_op jit(solution)/shard_map/while/body/eval_jaxpr/jit(_take)/select_n | solution.py:124
  279.1 12.3 %bitcast_convert_fusion = bf16[8,16,128,128]{3,2,1,0:T(8,128)(2,1)} fusion(bf16[8,16,3,128,128]{4,3,0,2,1:T(8,128)(2,1)} %bitcast.110, bf16[8,16,3,128,128]{4,3,0,2,1:T(8,128)(2,1)} %bitcast.109, bf16[16,3]{1,0:T(8,128)(2,1)S(1)} %convert_convert_fusion), kind=kOutput, calls=%fused_computation.40 | convolution fusion | flops 1619001344 | bytes 29360224 | tf_op jit(solution)/shard_map/while/body/eval_jaxpr/gtkia,gtkja->gtij/dot_general | solution.py:127
  291.4 4.7 %copy.33 = bf16[8,16,128,128]{3,2,0,1:T(8,128)(2,1)} copy(bf16[8,16,128,128]{3,2,1,0:T(8,128)(2,1)} %bitcast_convert_fusion) | data formatting | bytes 8388608 | tf_op jit(solution)/shard_map/while/body/eval_jaxpr/convert_element_type | solution.py:130
  296.2 4.9 %all-to-all-start.2 = ((bf16[8,16,128,128]{3,2,0,1:T(8,128)(2,1)}), bf16[8,16,128,128]{3,2,0,1:T(8,128)(2,1)}, u32[]{:S(2)}, u32[]{:S(2)}) async-start(bf16[8,16,128,128]{3,2,0,1:T(8,128)(2,1)} %copy.33), calls=%async_computation.2 | async-start | bytes 8388608 | tf_op jit(solution)/shard_map/all_to_all | solution.py:134
  301.1 7.8 %fusion.3 = f32[16384,128]{1,0:T(8,128)} fusion(bf16[16384,128]{1,0:T(8,128)(2,1)} %copy-done.1, bf16[128,128]{1,0:T(8,128)(2,1)S(1)} %copy-done), kind=kOutput, calls=%fused_computation.9 | convolution fusion | flops 543162368 | bytes 12615680 | tf_op jit(solution)/shard_map/dot_general | solution.py:98
  308.9 84.7 %all-to-all-done.2 = bf16[8,16,128,128]{3,2,0,1:T(8,128)(2,1)} async-done(((bf16[8,16,128,128]{3,2,0,1:T(8,128)(2,1)}), bf16[8,16,128,128]{3,2,0,1:T(8,128)(2,1)}, u32[]{:S(2)}, u32[]{:S(2)}) %all-to-all-start.2) | async-done | bytes 4194336 | tf_op jit(solution)/shard_map/all_to_all | solution.py:134
  403.4 11.4 %fusion.2 = bf16[16384,128]{1,0:T(8,128)(2,1)} fusion(f32[16384,128]{1,0:T(8,128)S(1)} %bitcast.112, bf16[128,128]{1,0:T(8,128)(2,1)S(1)} %copy-done.4, f32[16,8,128,128]{3,2,1,0:T(8,128)S(1)} %convert_bitcast_fusion, f32[128]{0:T(128)S(1)} %copy-done.8, f32[128]{0:T(128)S(1)} %copy-done.9, f32[16384]{0:T(1024)S(1)} %rsqrt_bitcast_fusion, ...), kind=kOutput, calls=%fused_computation.8 | convolution fusion | flops 551550976 | bytes 21136384 | tf_op jit(solution)/shard_map/dot_general | solution.py:142
  (61 shorter events, 16.4 us)
Async XLA Ops:
  0.0 301.1 %copy-start = (bf16[128,128]{1,0:T(8,128)(2,1)S(1)}, bf16[128,128]{1,0:T(8,128)(2,1)}, u32[]{:S(2)}) copy-start(bf16[128,128]{1,0:T(8,128)(2,1)} %param.18) | copy-start | bytes 98308
  0.0 9.6 %copy-start.2 = (bf16[1,128,128,128]{3,2,1,0:T(8,128)(2,1)S(1)}, bf16[1,128,128,128]{3,2,1,0:T(8,128)(2,1)}, u32[]{:S(2)}) copy-start(bf16[1,128,128,128]{3,2,1,0:T(8,128)(2,1)} %param.12) | copy-start | bytes 12582916
  0.0 9.6 %copy-start.7 = (f32[128]{0:T(128)S(1)}, f32[128]{0:T(128)}, u32[]{:S(2)}) copy-start(f32[128]{0:T(128)} %param.15) | copy-start | bytes 1540
  0.0 9.6 %copy-start.6 = (f32[128]{0:T(128)S(1)}, f32[128]{0:T(128)}, u32[]{:S(2)}) copy-start(f32[128]{0:T(128)} %param.16) | copy-start | bytes 1540
  0.0 14.6 %copy-start.3 = (bf16[128,512]{1,0:T(8,128)(2,1)S(1)}, bf16[128,512]{1,0:T(8,128)(2,1)}, u32[]{:S(2)}) copy-start(bf16[128,512]{1,0:T(8,128)(2,1)} %param.17) | copy-start | bytes 393220
  14.6 8.0 %copy-start.1 = (bf16[16384,128]{1,0:T(8,128)(2,1)}, bf16[16384,128]{1,0:T(8,128)(2,1)S(1)}, u32[]{:S(2)}) copy-start(bf16[16384,128]{1,0:T(8,128)(2,1)S(1)} %fusion.27) | copy-start | bytes 12582916
  22.7 8.0 %copy-start.10 = (s32[2]{0:T(128)S(1)}, s32[2]{0:T(128)}, u32[]{:S(2)}) copy-start(s32[2]{0:T(128)} %param.13) | copy-start | bytes 28
  22.7 8.5 %copy-start.5 = (s32[16]{0:T(128)S(1)}, s32[16]{0:T(128)}, u32[]{:S(2)}) copy-start(s32[16]{0:T(128)} %param.14) | copy-start | bytes 196
  63.4 99.0 %all-to-all-start = ((bf16[16,8,1,128,128]{4,3,1,2,0:T(8,128)(2,1)}), bf16[16,8,1,128,128]{4,3,1,2,0:T(8,128)(2,1)}, u32[]{:S(2)}, u32[]{:S(2)}) async-start(bf16[16,8,1,128,128]{4,3,1,2,0:T(8,128)(2,1)} %bitcast.106), calls=%async_computation | async-start | bytes 8388608 | tf_op jit(solution)/shard_map/all_to_all | solution.py:110
  162.5 97.4 %all-to-all-start.1 = ((bf16[16,8,1,128,128]{4,3,1,2,0:T(8,128)(2,1)}), bf16[16,8,1,128,128]{4,3,1,2,0:T(8,128)(2,1)}, u32[]{:S(2)}, u32[]{:S(2)}) async-start(bf16[16,8,1,128,128]{4,3,1,2,0:T(8,128)(2,1)} %bitcast.105), calls=%async_computation.1 | async-start | bytes 8388608 | tf_op jit(solution)/shard_map/all_to_all | solution.py:111
  296.2 97.4 %all-to-all-start.2 = ((bf16[8,16,128,128]{3,2,0,1:T(8,128)(2,1)}), bf16[8,16,128,128]{3,2,0,1:T(8,128)(2,1)}, u32[]{:S(2)}, u32[]{:S(2)}) async-start(bf16[8,16,128,128]{3,2,0,1:T(8,128)(2,1)} %copy.33), calls=%async_computation.2 | async-start | bytes 8388608 | tf_op jit(solution)/shard_map/all_to_all | solution.py:134
  396.4 7.0 %slice-start = ((s8[8388608]{0:T(1024)(128)(4,1)}), s8[4194304]{0:T(1024)(128)(4,1)S(1)}, s32[]{:S(2)}) async-start(s8[8388608]{0:T(1024)(128)(4,1)} %bitcast.111), calls=%async_computation.3 | async-start | bytes 8388608
  396.4 7.0 %copy-start.4 = (bf16[128,128]{1,0:T(8,128)(2,1)S(1)}, bf16[128,128]{1,0:T(8,128)(2,1)}, u32[]{:S(2)}) copy-start(bf16[128,128]{1,0:T(8,128)(2,1)} %param.21) | copy-start | bytes 98308
  396.4 7.0 %copy-start.8 = (f32[128]{0:T(128)S(1)}, f32[128]{0:T(128)}, u32[]{:S(2)}) copy-start(f32[128]{0:T(128)} %param.20) | copy-start | bytes 1540
  396.4 6.9 %copy-start.9 = (f32[128]{0:T(128)S(1)}, f32[128]{0:T(128)}, u32[]{:S(2)}) copy-start(f32[128]{0:T(128)} %param.19) | copy-start | bytes 1540
  399.9 3.5 slice-start.1
where the time goes:
time: 416 us; the launch traced here: 415 us
  waiting for transfers between devices  238 us (57%)
  other arithmetic  64.4 us (15%)
  local copies, waits for them, and re-layouts  48.3 us (12%)
  matrix products  47.6 us (11%)
  starting transfers between devices  16.4 us (4%)
    all_to_all x1, waiting for transfers between devices, shards(): lax.all_to_all(mixed, 'row', split_axis=1, concat_axis=0, tiled=True)  84.7 us
    all_to_all x1, waiting for transfers between devices, shards(): lax.all_to_all(left_tiles, 'row', split_axis=0, concat_axis=2, tiled=True)  80.7 us
    all_to_all x1, waiting for transfers between devices, shards(): lax.all_to_all(right_tiles, 'row', split_axis=0, concat_axis=2, tiled=True)  72.5 us
    dot_general x2, matrix products, operand(): lax.dot_general(weights, normed, (((0,), (1,)), ((), ())), preferred_elem...  16.1 us
    convert_element_type x1, other arithmetic, operand(): result.astype(jnp.bfloat16)  15 us
    convert_element_type x2, local copies, waits for them, and re-layouts, operand(): result.astype(jnp.bfloat16)  12.8 us
    dot_general x1, matrix products, one_block(): jnp.einsum('gtkia,gtkja->gtij', picked_left, picked_right, preferred_elem...  12.3 us
    dot_general x1, matrix products, shards(): lax.dot_general(mixed_norm, out_weight, (((0,), (0,)), ((), ())), preferr...  11.4 us
  transfers between devices with their start and end apart: 3, of which 3 were waited for; matrix products, arithmetic and copies ran while one was open for 10% of the time, Pallas kernels for 0%

commit v1 on v0

v1 whole, which is shorter than its diff:
```python
import functools
import jax
import jax.numpy as jnp
from jax import lax
from jax.experimental import pallas as pl
from jax.experimental.pallas import tpu as pltpu
from jax.sharding import PartitionSpec as P

ROWS = 32


def pick_slot(onehot, values):
    return jnp.sum(jnp.where(onehot, values[None, :], 0), 1)


def tile_tables(comp_len, tile_place, tiles, tile_side, most_tiles):
    counts = (comp_len + tile_side - 1) // tile_side
    areas = counts * counts
    starts = jnp.cumsum(areas) - areas
    numbers = jnp.arange(tiles, dtype=jnp.int32)
    inside = (
        (numbers[:, None] >= starts[None, :]) & (numbers[:, None] < (starts + areas)[None, :])
    ).astype(jnp.int32)
    used = jnp.sum(inside, 1)
    sides = jnp.sum(inside * counts[None, :], 1)
    firsts = jnp.sum(inside * starts[None, :], 1)
    lengths = jnp.sum(inside * comp_len[None, :], 1)
    local_number = numbers - firsts
    safe_side = jnp.maximum(sides, 1)
    tile_row = local_number // safe_side
    tile_col = local_number % safe_side
    onehot = tile_place[None, :] == numbers[:, None]
    slot_used = pick_slot(onehot, used)
    slot_side = pick_slot(onehot, sides)
    slot_first = pick_slot(onehot, firsts)
    slot_length = pick_slot(onehot, lengths)
    slot_row = pick_slot(onehot, tile_row)
    slot_col = pick_slot(onehot, tile_col)
    steps_k = jnp.arange(most_tiles, dtype=jnp.int32)
    left_number = jnp.clip(
        slot_first[:, None] + slot_row[:, None] * slot_side[:, None] + steps_k[None, :],
        0,
        tiles - 1,
    )
    right_number = jnp.clip(
        slot_first[:, None] + slot_col[:, None] * slot_side[:, None] + steps_k[None, :],
        0,
        tiles - 1,
    )
    left_slot = jnp.sum(
        jnp.where(left_number[:, :, None] == numbers[None, None, :], tile_place[None, None, :], 0),
        2,
    )
    right_slot = jnp.sum(
        jnp.where(right_number[:, :, None] == numbers[None, None, :], tile_place[None, None, :], 0),
        2,
    )
    valid = ((steps_k[None, :] < slot_side[:, None]) & (slot_used[:, None] > 0)).astype(jnp.float32)
    own = (numbers == lax.axis_index("row")).astype(jnp.int32)
    own_length = jnp.sum(own * slot_length * slot_used)
    rows_left = own_length - jnp.sum(own * slot_row) * tile_side
    cols_left = own_length - jnp.sum(own * slot_col) * tile_side
    return (left_slot, right_slot, valid, jnp.stack([rows_left, cols_left]).astype(jnp.int32))


def kernel(
    n,
    most_tiles,
    left_slot,
    right_slot,
    valid,
    live,
    pair,
    in_gain,
    in_bias,
    proj_weight,
    gate_weight,
    out_gain,
    out_bias,
    out_weight,
    update,
    weights_t,
    gain_cols,
    bias_cols,
    stage,
    right_send,
    right_recv,
    left_send,
    mixed_send,
    mixed_recv,
    right_sems,
    left_send_sems,
    left_recv_sems,
    mixed_send_sems,
    mixed_recv_sems,
    own_sems,
    *left_recv,
):
    side = pair.shape[0]
    channels = out_weight.shape[0]
    group = channels // n
    chunks = side // ROWS
    me = lax.axis_index("row")

    barrier = pltpu.get_barrier_semaphore()

    @pl.loop(1, n)
    def _(step):
        peer = lax.rem(me + step, n)
        pl.semaphore_signal(
            barrier, inc=1, device_id={"row": peer}, device_id_type=pl.DeviceIdType.MESH
        )

    weights_t[...] = proj_weight[...].astype(jnp.float32).T.astype(jnp.bfloat16)
    gain_cols[...] = jnp.broadcast_to(out_gain[...], (side, channels)).T
    bias_cols[...] = jnp.broadcast_to(out_bias[...], (side, channels)).T

    def normalize(row):
        values = pair[row].astype(jnp.float32)
        average = jnp.mean(values, 1, keepdims=True)
        centred = values - average
        variance = jnp.mean(centred * centred, 1, keepdims=True)
        scaled = centred * lax.rsqrt(variance + 1e-05)
        return (scaled * in_gain[...] + in_bias[...]).astype(jnp.bfloat16)

    def project(which, chunk, send):
        cols = lax.broadcasted_iota(jnp.int32, (1, side), 1)
        cols_ok = (cols < live[1]).astype(jnp.float32)

        def one_row(row, carry):
            normed = normalize(chunk * ROWS + row)
            projected = lax.dot_general(
                weights_t[pl.ds(2 * which * channels, 2 * channels), :],
                normed,
                (((1,), (1,)), ((), ())),
                preferred_element_type=jnp.float32,
            )
            row_ok = (chunk * ROWS + row < live[0]).astype(jnp.float32)
            result = cols_ok * row_ok * jax.nn.sigmoid(projected[:channels]) * projected[channels:]
            stage[pl.ds(row, channels, stride=ROWS), :] = result
            return carry

        lax.fori_loop(0, ROWS, one_row, 0, unroll=2)

        def one_peer(peer, carry):
            for g in range(group):
                first = pl.multiple_of((peer * group + g) * ROWS, ROWS)
                send[peer, g, pl.ds(chunk * ROWS, ROWS), :] = stage[pl.ds(first, ROWS), :].astype(
                    jnp.bfloat16
                )
            return carry

        lax.fori_loop(0, n, one_peer, 0)

    def remote(src, dst, send_sem, recv_sem, peer):
        return pltpu.make_async_remote_copy(
            src_ref=src,
            dst_ref=dst,
            send_sem=send_sem,
            recv_sem=recv_sem,
            device_id={"row": peer},
            device_id_type=pl.DeviceIdType.MESH,
        )

    def wait_bytes(ref, sem):
        pltpu.make_async_copy(ref, ref, sem).wait()

    for chunk in range(chunks):
        rows = pl.ds(chunk * ROWS, ROWS)
        project(1, chunk, right_send)
        if chunk == 0:
            pl.semaphore_wait(barrier, n - 1)

        @pl.loop(1, n)
        def _(step):
            peer = lax.rem(me + step, n)
            remote(
                right_send.at[peer, :, rows, :],
                right_recv.at[me, :, rows, :],
                right_sems.at[0],
                right_sems.at[1],
                peer,
            ).start()

    own_right = pltpu.make_async_copy(right_send.at[me], right_recv.at[me], own_sems.at[0])
    own_right.start()

    own_left = []
    for chunk in range(chunks):
        rows = pl.ds(chunk * ROWS, ROWS)
        project(0, chunk, left_send)

        @pl.loop(1, n)
        def _(step):
            peer = lax.rem(me + step, n)
            remote(
                left_send.at[peer, :, rows, :],
                left_recv[chunk].at[me],
                left_send_sems.at[0],
                left_recv_sems.at[chunk],
                peer,
            ).start()

        copy = pltpu.make_async_copy(
            left_send.at[me, :, rows, :], left_recv[chunk].at[me], own_sems.at[1 + chunk]
        )
        copy.start()
        own_left.append(copy)

    own_right.wait()
    wait_bytes(right_recv.at[pl.ds(0, n - 1)], right_sems.at[1])

    for chunk in range(chunks):
        own_left[chunk].wait()
        wait_bytes(left_recv[chunk].at[pl.ds(0, n - 1)], left_recv_sems.at[chunk])

        def product(tile):
            for g in range(group):
                total = jnp.zeros((ROWS, side), jnp.float32)
                for k in range(most_tiles):
                    entry = tile * most_tiles + k
                    part = lax.dot_general(
                        left_recv[chunk][left_slot[entry], g],
                        right_recv[right_slot[entry], g],
                        (((1,), (1,)), ((), ())),
                        preferred_element_type=jnp.float32,
                    )
                    total = total + part * valid[entry]
                mixed_send[chunk, tile, g] = total.astype(jnp.bfloat16)

        @pl.loop(1, n)
        def _(step):
            tile = lax.rem(me + step, n)
            product(tile)
            remote(
                mixed_send.at[chunk, tile],
                mixed_recv.at[chunk, me],
                mixed_send_sems.at[0],
                mixed_recv_sems.at[chunk],
                tile,
            ).start()

        product(me)
        pltpu.make_async_copy(
            mixed_send.at[chunk, me], mixed_recv.at[chunk, me], own_sems.at[1 + chunks + chunk]
        ).start()

    for chunk in range(chunks):
        pltpu.make_async_copy(
            mixed_send.at[chunk, me], mixed_recv.at[chunk, me], own_sems.at[1 + chunks + chunk]
        ).wait()
        wait_bytes(mixed_recv.at[chunk, pl.ds(0, n - 1)], mixed_recv_sems.at[chunk])

        def unpack(source, carry):
            for g in range(group):
                first = pl.multiple_of((source * group + g) * ROWS, ROWS)
                stage[pl.ds(first, ROWS), :] = mixed_recv[chunk, source, g].astype(jnp.float32)
            return carry

        lax.fori_loop(0, n, unpack, 0)

        def finish(row, carry):
            values = stage[pl.ds(row, channels, stride=ROWS), :]
            average = jnp.mean(values, 0, keepdims=True)
            centred = values - average
            variance = jnp.mean(centred * centred, 0, keepdims=True)
            scaled = centred * lax.rsqrt(variance + 1e-05)
            mixed_norm = (scaled * gain_cols[...] + bias_cols[...]).T.astype(jnp.bfloat16)
            projected = jnp.dot(mixed_norm, out_weight[...], preferred_element_type=jnp.float32)
            normed = normalize(chunk * ROWS + row)
            gating = jax.nn.sigmoid(
                jnp.dot(normed, gate_weight[...], preferred_element_type=jnp.float32)
            )
            update[chunk * ROWS + row] = (gating * projected).astype(jnp.bfloat16)
            return carry

        lax.fori_loop(0, ROWS, finish, 0, unroll=2)

    wait_bytes(right_send.at[pl.ds(0, n - 1)], right_sems.at[0])
    wait_bytes(left_send.at[pl.ds(0, n - 1)], left_send_sems.at[0])
    wait_bytes(mixed_send.at[:, pl.ds(0, n - 1)], mixed_send_sems.at[0])


def shards(
    pair,
    comp_len,
    tile_place,
    in_gain,
    in_bias,
    proj_weight,
    gate_weight,
    out_gain,
    out_bias,
    out_weight,
):
    tiles = tile_place.shape[0]
    side = pair.shape[1]
    width = pair.shape[3]
    channels = out_weight.shape[0]
    n = lax.axis_size("row")
    group = channels // n
    most_tiles = 2 + tiles // 16
    chunks = side // ROWS
    left_slot, right_slot, valid, live = tile_tables(
        comp_len, tile_place, tiles, side, most_tiles
    )
    vmem = pl.BlockSpec(memory_space=pltpu.VMEM)
    smem = pl.BlockSpec(memory_space=pltpu.SMEM)
    result = pl.pallas_call(
        functools.partial(kernel, n, most_tiles),
        out_shape=jax.ShapeDtypeStruct((side, side, width), jnp.bfloat16),
        in_specs=[smem] * 4 + [vmem] * 8,
        out_specs=vmem,
        scratch_shapes=[
            pltpu.VMEM((4 * channels, width), jnp.bfloat16),
            pltpu.VMEM((channels, side), jnp.float32),
            pltpu.VMEM((channels, side), jnp.float32),
            pltpu.VMEM((channels * ROWS, side), jnp.float32),
            pltpu.VMEM((n, group, side, side), jnp.bfloat16),
            pltpu.VMEM((n, group, side, side), jnp.bfloat16),
            pltpu.VMEM((n, group, side, side), jnp.bfloat16),
            pltpu.VMEM((chunks, n, group, ROWS, side), jnp.bfloat16),
            pltpu.VMEM((chunks, n, group, ROWS, side), jnp.bfloat16),
            pltpu.SemaphoreType.DMA((2,)),
            pltpu.SemaphoreType.DMA((1,)),
            pltpu.SemaphoreType.DMA((chunks,)),
            pltpu.SemaphoreType.DMA((1,)),
            pltpu.SemaphoreType.DMA((chunks,)),
            pltpu.SemaphoreType.DMA((1 + 2 * chunks,)),
        ]
        + [pltpu.VMEM((n, group, ROWS, side), jnp.bfloat16)] * chunks,
        compiler_params=pltpu.CompilerParams(
            collective_id=0, has_side_effects=True, vmem_limit_bytes=56 * 1024 * 1024
        ),
    )(
        left_slot.reshape(-1),
        right_slot.reshape(-1),
        valid.reshape(-1),
        live,
        pair[0],
        in_gain[None, :],
        in_bias[None, :],
        proj_weight,
        gate_weight,
        out_gain[None, :],
        out_bias[None, :],
        out_weight,
    )
    return result[None]


def solution(mesh):
    placed = (
        P(("groups", "row"), None, None, None),
        P("groups"),
        P("groups"),
        P(),
        P(),
        P(),
        P(),
        P(),
        P(),
        P(),
    )
    return jax.shard_map(
        shards,
        mesh=mesh,
        in_specs=placed,
        out_specs=P(("groups", "row"), None, None, None),
        check_vma=False,
    )
```

time: 416 us -> 306 us (0.74)
  Pallas kernels: 0 us -> 292 us
  waiting for transfers between devices: 238 us -> 0 us
  other arithmetic: 64.4 us -> 4.92 us
  matrix products: 47.6 us -> 0 us
  local copies, waits for them, and re-layouts: 48.3 us -> 6.88 us
  starting transfers between devices: 16.4 us -> 0 us
    pallas_call x0 -> x1, Pallas kernels: none -> 292 us  [shards(): pl.pallas_call(functools.partial(kernel, n, most_tiles), out_shape=jax.Sh...]
    all_to_all x3 -> x0, waiting for transfers between devices: 238 us -> none  [the longest x1 84.7 us: shards(): lax.all_to_all(mixed, 'row', split_axis=1, concat_axis=0, tiled=True)]
    dot_general x5 -> x0, matrix products: 47.6 us -> none  [the longest x2 16.1 us: operand(): lax.dot_general(weights, normed, (((0,), (1,)), ((), ())), preferred_elem...]
    select_n x4 -> x0, other arithmetic: 21.5 us -> none  [the longest x2 10.8 us: one_block(): jnp.take(right_group, right_list, axis=1)]
    convert_element_type x3 -> x1, other arithmetic: 20.1 us -> 0.07 us  [tile_tables(): ((steps_k[None, :] < slot_side[:, None]) & (slot_used[:, None] > 0)).asty...]
    gather x2 -> x0, local copies, waits for them, and re-layouts: 17 us -> none  [the longest x1 8.55 us: one_block(): jnp.take(right_group, right_list, axis=1)]
    convert_element_type x3 -> x1, local copies, waits for them, and re-layouts: 17.5 us -> 0.68 us  [tile_tables(): ((steps_k[None, :] < slot_side[:, None]) & (slot_used[:, None] > 0)).asty...]
    all_to_all x3 -> x0, starting transfers between devices: 16.4 us -> none  [the longest x1 6.55 us: shards(): lax.all_to_all(left_tiles, 'row', split_axis=0, concat_axis=2, tiled=True)]
  transfers between devices with their start and end apart: 3 -> 0, of which waited for: 3 -> 0; matrix products, arithmetic and copies ran while one was open for 10% -> 0% of each run, Pallas kernels for 0% -> 0%
where the time goes in v1:
time: 306 us
  Pallas kernels  292 us (95%)
  local copies, waits for them, and re-layouts  6.88 us (2%)
  other arithmetic  4.92 us (2%)
    pallas_call x1, Pallas kernels, shards(): pl.pallas_call(functools.partial(kernel, n, most_tiles), out_shape=jax.Sh...  292 us

profile of v1, /device:TPU:15, one launch (start us, length us, event | category | flops | bytes accessed | tf_op | source)
XLA Modules:
  0.0 306.2 jit_solution(1954567898492984765)
XLA Ops:
  0.0 0.7 multiply_bitcast_fusion
  0.7 0.2 reduce-window.8
  0.9 0.7 select_reduce_fusion.8
  1.6 0.1 and_select_fusion.1
  1.7 0.8 select_reduce_fusion.2
  2.6 0.8 multiply_add_fusion.1
  5.9 0.6 pad_add_fusion.live
  6.5 0.9 select_reduce_fusion
  7.5 0.1 copy.12
  7.5 0.6 reshape.148.right_slot
  8.2 0.1 fusion.1
  8.3 0.7 reshape.149.valid
  8.9 0.1 copy.11
  9.0 0.6 reshape.147.left_slot
  9.6 291.8 %shard_map.100 = bf16[128,128,128]{2,1,0:T(8,128)(2,1)} custom-call(s32[48]{0:T(128)} %reshape.147.left_slot, s32[48]{0:T(128)} %reshape.148.right_slot, f32[48]{0:T(128)} %reshape.149.valid, s32[2]{0:T(128)} %pad_add_fusion.live, bf16[128,128,128]{2,1,0:T(8,128)(2,1)} %bitcast.13, f32[1,128]{1,0:T(1,128)} %bitcast.15, f32[1,128]{1,0:T(1,128)} %bitcast.16, ...), custom_call_target="tpu_custom_call" | custom-call | tf_op jit(solution)/shard_map/pallas_call | solution.py:309
  301.4 4.8 %copy.14 = bf16[1,128,128,128]{3,2,1,0:T(8,128)(2,1)} copy(bf16[1,128,128,128]{3,2,1,0:T(8,128)(2,1)} %bitcast.12) | data formatting | bytes 8388608
  (4 shorter events, 0.0 us)

commit v2 on v1

v2 whole, which is shorter than its diff:
```python
import functools
import jax
import jax.numpy as jnp
from jax import lax
from jax.experimental import pallas as pl
from jax.experimental.pallas import tpu as pltpu
from jax.sharding import PartitionSpec as P

RIGHT_PARTS = (16, 16, 32, 64)
LEFT_PARTS = (32, 32, 32, 16, 16)


def spans(parts):
    first = 0
    for rows in parts:
        yield (first, rows)
        first += rows


def kernel(
    n,
    most_tiles,
    comp_len,
    tile_place,
    pair_hbm,
    in_gain,
    in_bias,
    proj_weight,
    gate_weight,
    out_gain,
    out_bias,
    out_weight,
    update_hbm,
    left_slot,
    right_slot,
    valid,
    pair,
    update,
    weights_t,
    gain_cols,
    bias_cols,
    stage,
    right_send,
    right_recv,
    left_send,
    right_sems,
    left_send_sems,
    left_recv_sems,
    mixed_send_sems,
    mixed_recv_sems,
    own_sems,
    pair_sems,
    update_sems,
    *parts,
):
    chunks = len(LEFT_PARTS)
    left_recv = parts[:chunks]
    mixed_send = parts[chunks : 2 * chunks]
    mixed_recv = parts[2 * chunks :]
    side = pair.shape[0]
    channels = out_weight.shape[0]
    group = channels // n
    me = lax.axis_index("row")

    pair_copies = []
    for index, (first, rows) in enumerate(spans(RIGHT_PARTS)):
        copy = pltpu.make_async_copy(
            pair_hbm.at[pl.ds(first, rows)], pair.at[pl.ds(first, rows)], pair_sems.at[index]
        )
        copy.start()
        pair_copies.append(copy)

    barrier = pltpu.get_barrier_semaphore()

    @pl.loop(1, n)
    def _(step):
        peer = lax.rem(me + step, n)
        pl.semaphore_signal(
            barrier, inc=1, device_id={"row": peer}, device_id_type=pl.DeviceIdType.MESH
        )

    def peer_at(position):
        half = position // 2
        step = jnp.where(position % 2 == 0, n // 2 + half, half + 1)
        return lax.rem(me + step, n)

    def describe(slot):
        number = lax.fori_loop(
            0, n, lambda t, found: found + jnp.where(tile_place[t] == slot, t, 0), 0, unroll=4
        )
        start, first, count_in, length = 0, 0, 0, 0
        for c in range(comp_len.shape[0]):
            count = lax.div(comp_len[c] + (side - 1), side)
            inside = (number >= start) & (number < start + count * count)
            first = jnp.where(inside, start, first)
            count_in = jnp.where(inside, count, count_in)
            length = jnp.where(inside, comp_len[c], length)
            start = start + count * count
        local = number - first
        row = 0
        for m in range(1, most_tiles):
            row = row + jnp.where(local >= m * count_in, 1, 0)
        return first, count_in, length, row, local - row * count_in

    _, _, own_length, own_row, own_col = describe(me)
    rows_left = own_length - own_row * side
    cols_left = own_length - own_col * side

    weights_t[...] = proj_weight[...].astype(jnp.float32).T.astype(jnp.bfloat16)

    def normalize(row):
        values = pair[row].astype(jnp.float32)
        average = jnp.mean(values, 1, keepdims=True)
        centred = values - average
        variance = jnp.mean(centred * centred, 1, keepdims=True)
        scaled = centred * lax.rsqrt(variance + 1e-05)
        return (scaled * in_gain[...] + in_bias[...]).astype(jnp.bfloat16)

    def project(which, begin, rows, send):
        cols = lax.broadcasted_iota(jnp.int32, (1, side), 1)
        cols_ok = (cols < cols_left).astype(jnp.float32)

        def one_row(row, carry):
            normed = normalize(begin + row)
            projected = lax.dot_general(
                weights_t[pl.ds(2 * which * channels, 2 * channels), :],
                normed,
                (((1,), (1,)), ((), ())),
                preferred_element_type=jnp.float32,
            )
            row_ok = (begin + row < rows_left).astype(jnp.float32)
            result = cols_ok * row_ok * jax.nn.sigmoid(projected[:channels]) * projected[channels:]
            stage[pl.ds(row, channels, stride=rows), :] = result
            return carry

        lax.fori_loop(0, rows, one_row, 0, unroll=2)

        def one_peer(peer, carry):
            for g in range(group):
                first = pl.multiple_of((peer * group + g) * rows, rows)
                send[peer, g, pl.ds(begin, rows), :] = stage[pl.ds(first, rows), :].astype(
                    jnp.bfloat16
                )
            return carry

        lax.fori_loop(0, n, one_peer, 0)

    def remote(src, dst, send_sem, recv_sem, peer):
        return pltpu.make_async_remote_copy(
            src_ref=src,
            dst_ref=dst,
            send_sem=send_sem,
            recv_sem=recv_sem,
            device_id={"row": peer},
            device_id_type=pl.DeviceIdType.MESH,
        )

    def wait_bytes(ref, sem):
        pltpu.make_async_copy(ref, ref, sem).wait()

    for index, (begin, rows) in enumerate(spans(RIGHT_PARTS)):
        pair_copies[index].wait()
        project(1, begin, rows, right_send)
        if index == 0:
            pl.semaphore_wait(barrier, n - 1)

        @pl.loop(0, n - 1)
        def _(position):
            peer = peer_at(position)
            remote(
                right_send.at[peer, :, pl.ds(begin, rows), :],
                right_recv.at[me, :, pl.ds(begin, rows), :],
                right_sems.at[0],
                right_sems.at[1],
                peer,
            ).start()

    own_right = pltpu.make_async_copy(right_send.at[me], right_recv.at[me], own_sems.at[0])
    own_right.start()

    own_left = []
    for chunk, (begin, rows) in enumerate(spans(LEFT_PARTS)):
        project(0, begin, rows, left_send)

        @pl.loop(0, n - 1)
        def _(position):
            peer = peer_at(position)
            remote(
                left_send.at[peer, :, pl.ds(begin, rows), :],
                left_recv[chunk].at[me],
                left_send_sems.at[0],
                left_recv_sems.at[chunk],
                peer,
            ).start()

        copy = pltpu.make_async_copy(
            left_send.at[me, :, pl.ds(begin, rows), :],
            left_recv[chunk].at[me],
            own_sems.at[1 + chunk],
        )
        copy.start()
        own_left.append(copy)

    gain_cols[...] = jnp.broadcast_to(out_gain[...], (side, channels)).T
    bias_cols[...] = jnp.broadcast_to(out_bias[...], (side, channels)).T

    @pl.loop(0, n)
    def _(slot):
        first, count, _, row, col = describe(slot)
        for k in range(most_tiles):
            entry = slot * most_tiles + k
            left_slot[entry] = tile_place[jnp.clip(first + row * count + k, 0, n - 1)]
            right_slot[entry] = tile_place[jnp.clip(first + col * count + k, 0, n - 1)]
            valid[entry] = (k < count).astype(jnp.float32)

    own_right.wait()
    wait_bytes(right_recv.at[pl.ds(0, n - 1)], right_sems.at[1])

    own_mixed = []
    for chunk, (begin, rows) in enumerate(spans(LEFT_PARTS)):
        own_left[chunk].wait()
        wait_bytes(left_recv[chunk].at[pl.ds(0, n - 1)], left_recv_sems.at[chunk])

        def product(tile):
            for g in range(group):
                total = jnp.zeros((rows, side), jnp.float32)
                for k in range(most_tiles):
                    entry = tile * most_tiles + k
                    part = lax.dot_general(
                        left_recv[chunk][left_slot[entry], g],
                        right_recv[right_slot[entry], g],
                        (((1,), (1,)), ((), ())),
                        preferred_element_type=jnp.float32,
                    )
                    total = total + part * valid[entry]
                mixed_send[chunk][tile, g] = total.astype(jnp.bfloat16)

        @pl.loop(0, n - 1)
        def _(position):
            tile = peer_at(position)
            product(tile)
            remote(
                mixed_send[chunk].at[tile],
                mixed_recv[chunk].at[me],
                mixed_send_sems.at[chunk],
                mixed_recv_sems.at[chunk],
                tile,
            ).start()

        product(me)
        copy = pltpu.make_async_copy(
            mixed_send[chunk].at[me], mixed_recv[chunk].at[me], own_sems.at[1 + chunks + chunk]
        )
        copy.start()
        own_mixed.append(copy)

    update_copies = []
    for chunk, (begin, rows) in enumerate(spans(LEFT_PARTS)):
        own_mixed[chunk].wait()
        wait_bytes(mixed_recv[chunk].at[pl.ds(0, n - 1)], mixed_recv_sems.at[chunk])

        def unpack(source, carry):
            for g in range(group):
                first = pl.multiple_of((source * group + g) * rows, rows)
                stage[pl.ds(first, rows), :] = mixed_recv[chunk][source, g].astype(jnp.float32)
            return carry

        lax.fori_loop(0, n, unpack, 0)

        def finish(row, carry):
            values = stage[pl.ds(row, channels, stride=rows), :]
            average = jnp.mean(values, 0, keepdims=True)
            centred = values - average
            variance = jnp.mean(centred * centred, 0, keepdims=True)
            scaled = centred * lax.rsqrt(variance + 1e-05)
            mixed_norm = (scaled * gain_cols[...] + bias_cols[...]).T.astype(jnp.bfloat16)
            projected = jnp.dot(mixed_norm, out_weight[...], preferred_element_type=jnp.float32)
            normed = normalize(begin + row)
            gating = jax.nn.sigmoid(
                jnp.dot(normed, gate_weight[...], preferred_element_type=jnp.float32)
            )
            update[begin + row] = (gating * projected).astype(jnp.bfloat16)
            return carry

        lax.fori_loop(0, rows, finish, 0, unroll=2)
        copy = pltpu.make_async_copy(
            update.at[pl.ds(begin, rows)], update_hbm.at[pl.ds(begin, rows)], update_sems.at[chunk]
        )
        copy.start()
        update_copies.append(copy)

    wait_bytes(right_send.at[pl.ds(0, n - 1)], right_sems.at[0])
    wait_bytes(left_send.at[pl.ds(0, n - 1)], left_send_sems.at[0])
    for chunk in range(chunks):
        wait_bytes(mixed_send[chunk].at[pl.ds(0, n - 1)], mixed_send_sems.at[chunk])
        update_copies[chunk].wait()


def shards(
    pair,
    comp_len,
    tile_place,
    in_gain,
    in_bias,
    proj_weight,
    gate_weight,
    out_gain,
    out_bias,
    out_weight,
):
    tiles = tile_place.shape[0]
    side = pair.shape[1]
    width = pair.shape[3]
    channels = out_weight.shape[0]
    n = lax.axis_size("row")
    group = channels // n
    most_tiles = 2 + tiles // 16
    chunks = len(LEFT_PARTS)
    vmem = pl.BlockSpec(memory_space=pltpu.VMEM)
    smem = pl.BlockSpec(memory_space=pltpu.SMEM)
    hbm = pl.BlockSpec(memory_space=pl.ANY)
    by_part = [pltpu.VMEM((n, group, rows, side), jnp.bfloat16) for rows in LEFT_PARTS]
    result = pl.pallas_call(
        functools.partial(kernel, n, most_tiles),
        out_shape=jax.ShapeDtypeStruct((side, side, width), jnp.bfloat16),
        in_specs=[smem] * 2 + [hbm] + [vmem] * 7,
        out_specs=hbm,
        scratch_shapes=[
            pltpu.SMEM((n * most_tiles,), jnp.int32),
            pltpu.SMEM((n * most_tiles,), jnp.int32),
            pltpu.SMEM((n * most_tiles,), jnp.float32),
            pltpu.VMEM((side, side, width), jnp.bfloat16),
            pltpu.VMEM((side, side, width), jnp.bfloat16),
            pltpu.VMEM((4 * channels, width), jnp.bfloat16),
            pltpu.VMEM((channels, side), jnp.float32),
            pltpu.VMEM((channels, side), jnp.float32),
            pltpu.VMEM((channels * max(RIGHT_PARTS + LEFT_PARTS), side), jnp.float32),
            pltpu.VMEM((n, group, side, side), jnp.bfloat16),
            pltpu.VMEM((n, group, side, side), jnp.bfloat16),
            pltpu.VMEM((n, group, side, side), jnp.bfloat16),
            pltpu.SemaphoreType.DMA((2,)),
            pltpu.SemaphoreType.DMA((1,)),
            pltpu.SemaphoreType.DMA((chunks,)),
            pltpu.SemaphoreType.DMA((chunks,)),
            pltpu.SemaphoreType.DMA((chunks,)),
            pltpu.SemaphoreType.DMA((1 + 2 * chunks,)),
            pltpu.SemaphoreType.DMA((len(RIGHT_PARTS),)),
            pltpu.SemaphoreType.DMA((chunks,)),
        ]
        + by_part * 3,
        compiler_params=pltpu.CompilerParams(
            collective_id=0, has_side_effects=True, vmem_limit_bytes=56 * 1024 * 1024
        ),
    )(
        comp_len,
        tile_place,
        pair[0],
        in_gain[None, :],
        in_bias[None, :],
        proj_weight,
        gate_weight,
        out_gain[None, :],
        out_bias[None, :],
        out_weight,
    )
    return result[None]


def solution(mesh):
    placed = (
        P(("groups", "row"), None, None, None),
        P("groups"),
        P("groups"),
        P(),
        P(),
        P(),
        P(),
        P(),
        P(),
        P(),
    )
    return jax.shard_map(
        shards,
        mesh=mesh,
        in_specs=placed,
        out_specs=P(("groups", "row"), None, None, None),
        check_vma=False,
    )
```

time: 306 us -> 290 us (0.948); the launches traced: 306 us -> 287 us
  Pallas kernels: 292 us -> 282 us
  other arithmetic: 4.92 us -> 0 us
    pallas_call x1, Pallas kernels: 292 us -> 282 us  [shards(): pl.pallas_call(functools.partial(kernel, n, most_tiles), out_shape=jax.Sh...]
where the time goes in v2:
time: 290 us; the launch traced here: 287 us
  Pallas kernels  282 us (97%)
  local copies, waits for them, and re-layouts  4.79 us (2%)
    pallas_call x1, Pallas kernels, shards(): pl.pallas_call(functools.partial(kernel, n, most_tiles), out_shape=jax.Sh...  282 us

profile of v2, /device:TPU:15, one launch (start us, length us, event | category | flops | bytes accessed | tf_op | source)
XLA Modules:
  0.0 286.6 jit_solution(10717471758483341227)
XLA Ops:
  0.0 281.8 %shard_map.100 = bf16[128,128,128]{2,1,0:T(8,128)(2,1)} custom-call(s32[2]{0:T(128)} %comp_len.1, s32[16]{0:T(128)} %tile_place.1, bf16[128,128,128]{2,1,0:T(8,128)(2,1)} %bitcast.7, f32[1,128]{1,0:T(1,128)} %bitcast.8, f32[1,128]{1,0:T(1,128)} %bitcast.9, bf16[128,512]{1,0:T(8,128)(2,1)} %proj_weight.1, bf16[128,128]{1,0:T(8,128)(2,1)} %gate_weight.1, ...), custom_call_target="tpu_custom_call" | custom-call | tf_op jit(solution)/shard_map/pallas_call | solution.py:323
  281.8 4.8 %copy.12 = bf16[1,128,128,128]{3,2,1,0:T(8,128)(2,1)} copy(bf16[1,128,128,128]{3,2,1,0:T(8,128)(2,1)} %bitcast.6) | data formatting | bytes 8388608

commit v3 on v2

--- a/solution.py
+++ b/solution.py
@@ -8,6 +8,7 @@
 
 RIGHT_PARTS = (16, 16, 32, 64)
 LEFT_PARTS = (32, 32, 32, 16, 16)
+UNROLL = 4
 
 
 def spans(parts):
@@ -15,6 +16,88 @@
     for rows in parts:
         yield (first, rows)
         first += rows
+
+
+def normalize_row(values, gain, offset):
+    values = values.astype(jnp.float32)
+    average = jnp.mean(values, 1, keepdims=True)
+    centred = values - average
+    variance = jnp.mean(centred * centred, 1, keepdims=True)
+    scaled = centred * lax.rsqrt(variance + 1e-05)
+    return (scaled * gain + offset).astype(jnp.bfloat16)
+
+
+def unpack_mixed(mixed, stage, rows):
+    sources, group = mixed.shape[:2]
+
+    def unpack(source, carry):
+        for g in range(group):
+            first = pl.multiple_of((source * group + g) * rows, rows)
+            stage[pl.ds(first, rows), :] = mixed[source, g].astype(jnp.float32)
+        return carry
+
+    lax.fori_loop(0, sources, unpack, 0)
+
+
+def finish_row(values, gain_cols, bias_cols, out_weight, normed, gate_weight):
+    average = jnp.mean(values, 0, keepdims=True)
+    centred = values - average
+    variance = jnp.mean(centred * centred, 0, keepdims=True)
+    scaled = centred * lax.rsqrt(variance + 1e-05)
+    mixed_norm = (scaled * gain_cols + bias_cols).T.astype(jnp.bfloat16)
+    projected = jnp.dot(mixed_norm, out_weight, preferred_element_type=jnp.float32)
+    gating = jax.nn.sigmoid(jnp.dot(normed, gate_weight, preferred_element_type=jnp.float32))
+    return (gating * projected).astype(jnp.bfloat16)
+
+
+def finish_kernel(
+    partial,
+    mixed,
+    pair,
+    in_gain,
+    in_bias,
+    gate_weight,
+    out_gain,
+    out_bias,
+    out_weight,
+    update,
+    gain_cols,
+    bias_cols,
+    stage,
+    last,
+    sems,
+):
+    side = partial.shape[0]
+    channels = out_weight.shape[0]
+    rows = last.shape[0]
+    copies = []
+    for index in range(side // rows - 1):
+        span = pl.ds(index * rows, rows)
+        copies.append(pltpu.make_async_copy(partial.at[span], update.at[span], sems.at[index]))
+        copies[-1].start()
+    gain_cols[...] = jnp.broadcast_to(out_gain[...], (side, channels)).T
+    bias_cols[...] = jnp.broadcast_to(out_bias[...], (side, channels)).T
+    unpack_mixed(mixed, stage, rows)
+
+    def finish(row, carry):
+        last[row] = finish_row(
+            stage[pl.ds(row, channels, stride=rows), :],
+            gain_cols[...],
+            bias_cols[...],
+            out_weight[...],
+            normalize_row(pair[row], in_gain[...], in_bias[...]),
+            gate_weight[...],
+        )
+        return carry
+
+    lax.fori_loop(0, rows, finish, 0, unroll=UNROLL)
+    copy = pltpu.make_async_copy(
+        last, update.at[pl.ds(side - rows, rows)], sems.at[side // rows - 1]
+    )
+    copy.start()
+    for other in copies:
+        other.wait()
+    copy.wait()
 
 
 def kernel(
@@ -31,6 +114,7 @@
     out_bias,
     out_weight,
     update_hbm,
+    mixed_last,
     left_slot,
     right_slot,
     valid,
@@ -109,12 +193,7 @@
     weights_t[...] = proj_weight[...].astype(jnp.float32).T.astype(jnp.bfloat16)
 
     def normalize(row):
-        values = pair[row].astype(jnp.float32)
-        average = jnp.mean(values, 1, keepdims=True)
-        centred = values - average
-        variance = jnp.mean(centred * centred, 1, keepdims=True)
-        scaled = centred * lax.rsqrt(variance + 1e-05)
-        return (scaled * in_gain[...] + in_bias[...]).astype(jnp.bfloat16)
+        return normalize_row(pair[row], in_gain[...], in_bias[...])
 
     def project(which, begin, rows, send):
         cols = lax.broadcasted_iota(jnp.int32, (1, side), 1)
@@ -133,7 +212,7 @@
             stage[pl.ds(row, channels, stride=rows), :] = result
             return carry
 
-        lax.fori_loop(0, rows, one_row, 0, unroll=2)
+        lax.fori_loop(0, rows, one_row, 0, unroll=UNROLL)
 
         def one_peer(peer, carry):
             for g in range(group):
@@ -259,30 +338,26 @@
         own_mixed[chunk].wait()
         wait_bytes(mixed_recv[chunk].at[pl.ds(0, n - 1)], mixed_recv_sems.at[chunk])
 
-        def unpack(source, carry):
-            for g in range(group):
-                first = pl.multiple_of((source * group + g) * rows, rows)
-                stage[pl.ds(first, rows), :] = mixed_recv[chunk][source, g].astype(jnp.float32)
+        if chunk == chunks - 1:
+            copy = pltpu.make_async_copy(mixed_recv[chunk], mixed_last, update_sems.at[chunk])
+            copy.start()
+            update_copies.append(copy)
+            continue
+
+        unpack_mixed(mixed_recv[chunk], stage, rows)
+
+        def finish(row, carry):
+            update[begin + row] = finish_row(
+                stage[pl.ds(row, channels, stride=rows), :],
+                gain_cols[...],
+                bias_cols[...],
+                out_weight[...],
+                normalize(begin + row),
+                gate_weight[...],
+            )
             return carry
 
-        lax.fori_loop(0, n, unpack, 0)
-
-        def finish(row, carry):
-            values = stage[pl.ds(row, channels, stride=rows), :]
-            average = jnp.mean(values, 0, keepdims=True)
-            centred = values - average
-            variance = jnp.mean(centred * centred, 0, keepdims=True)
-            scaled = centred * lax.rsqrt(variance + 1e-05)
-            mixed_norm = (scaled * gain_cols[...] + bias_cols[...]).T.astype(jnp.bfloat16)
-            projected = jnp.dot(mixed_norm, out_weight[...], preferred_element_type=jnp.float32)
-            normed = normalize(begin + row)
-            gating = jax.nn.sigmoid(
-                jnp.dot(normed, gate_weight[...], preferred_element_type=jnp.float32)
-            )
-            update[begin + row] = (gating * projected).astype(jnp.bfloat16)
-            return carry
-
-        lax.fori_loop(0, rows, finish, 0, unroll=2)
+        lax.fori_loop(0, rows, finish, 0, unroll=UNROLL)
         copy = pltpu.make_async_copy(
             update.at[pl.ds(begin, rows)], update_hbm.at[pl.ds(begin, rows)], update_sems.at[chunk]
         )
@@ -320,11 +395,15 @@
     smem = pl.BlockSpec(memory_space=pltpu.SMEM)
     hbm = pl.BlockSpec(memory_space=pl.ANY)
     by_part = [pltpu.VMEM((n, group, rows, side), jnp.bfloat16) for rows in LEFT_PARTS]
-    result = pl.pallas_call(
+    last = LEFT_PARTS[-1]
+    partial, mixed_last = pl.pallas_call(
         functools.partial(kernel, n, most_tiles),
-        out_shape=jax.ShapeDtypeStruct((side, side, width), jnp.bfloat16),
+        out_shape=(
+            jax.ShapeDtypeStruct((side, side, width), jnp.bfloat16),
+            jax.ShapeDtypeStruct((n, group, last, side), jnp.bfloat16),
+        ),
         in_specs=[smem] * 2 + [hbm] + [vmem] * 7,
-        out_specs=hbm,
+        out_specs=(hbm, hbm),
         scratch_shapes=[
             pltpu.SMEM((n * most_tiles,), jnp.int32),
             pltpu.SMEM((n * most_tiles,), jnp.int32),
@@ -363,6 +442,36 @@
         out_bias[None, :],
         out_weight,
     )
+    result = pl.pallas_call(
+        finish_kernel,
+        grid=(1,),
+        out_shape=jax.ShapeDtypeStruct((side, side, width), jnp.bfloat16),
+        in_specs=[
+            hbm,
+            vmem,
+            pl.BlockSpec((last, side, width), lambda step: (side // last - 1, 0, 0)),
+        ]
+        + [vmem] * 6,
+        out_specs=hbm,
+        scratch_shapes=[
+            pltpu.VMEM((channels, side), jnp.float32),
+            pltpu.VMEM((channels, side), jnp.float32),
+            pltpu.VMEM((channels * last, side), jnp.float32),
+            pltpu.VMEM((last, side, width), jnp.bfloat16),
+            pltpu.SemaphoreType.DMA((side // last,)),
+        ],
+        compiler_params=pltpu.CompilerParams(vmem_limit_bytes=32 * 1024 * 1024),
+    )(
+        partial,
+        mixed_last,
+        pair[0],
+        in_gain[None, :],
+        in_bias[None, :],
+        gate_weight,
+        out_gain[None, :],
+        out_bias[None, :],
+        out_weight,
+    )
     return result[None]
 
 

time: 290 us -> 288 us (level)
    pallas_call x1 -> x2, Pallas kernels: 282 us -> 281 us  [the longest x1 278 us: shards(): pl.pallas_call(functools.partial(kernel, n, most_tiles), out_shape=(jax.S...]
where the time goes in v3:
time: 288 us; the launch traced here: 284 us
  Pallas kernels  281 us (98%)
  local copies, waits for them, and re-layouts  3.25 us (1%)
    pallas_call x1, Pallas kernels, shards(): pl.pallas_call(functools.partial(kernel, n, most_tiles), out_shape=(jax.S...  278 us

profile of v3, /device:TPU:15, one launch (start us, length us, event | category | flops | bytes accessed | tf_op | source)
XLA Modules:
  0.0 284.5 jit_solution(10578168399702446581)
XLA Ops:
  0.0 0.0 copy-start.4
  0.0 0.0 copy-start.3
  0.0 0.0 copy-start.8
  0.0 0.0 copy-start.7
  0.0 0.0 copy-start.6
  0.0 0.0 copy-start.5
  0.0 0.0 copy-start
  0.0 277.7 %shard_map.100 = (bf16[128,128,128]{2,1,0:T(8,128)(2,1)}, bf16[16,8,16,128]{3,2,1,0:T(8,128)(2,1)}) custom-call(s32[2]{0:T(128)} %comp_len.1, s32[16]{0:T(128)} %tile_place.1, bf16[128,128,128]{2,1,0:T(8,128)(2,1)} %bitcast.6, f32[1,128]{1,0:T(1,128)} %bitcast.8, f32[1,128]{1,0:T(1,128)} %bitcast.10, bf16[128,512]{1,0:T(8,128)(2,1)} %proj_weight.1, ...), custom_call_target="tpu_custom_call" | custom-call | tf_op jit(solution)/shard_map/pallas_call | solution.py:399
  277.8 0.0 copy-done.4
  277.8 0.0 copy-done.3
  277.8 0.0 copy-done.8
  277.8 0.0 copy-done.7
  277.8 0.0 copy-done.6
  277.8 0.0 copy-done.5
  277.8 0.0 copy-done
  277.8 0.0 copy-start.1
  277.8 2.2 copy-done.1
  280.0 0.0 copy-start.2
  280.0 1.0 copy-done.2
  281.1 3.4 %shard_map.101 = bf16[128,128,128]{2,1,0:T(8,128)(2,1)} custom-call(bf16[128,128,128]{2,1,0:T(8,128)(2,1)S(1)} %copy-done.1, bf16[16,8,16,128]{3,2,1,0:T(8,128)(2,1)S(1)} %copy-done.2, bf16[128,128,128]{2,1,0:T(8,128)(2,1)S(1)} %bitcast.7, f32[1,128]{1,0:T(1,128)S(1)} %bitcast.9, f32[1,128]{1,0:T(1,128)S(1)} %bitcast.11, bf16[128,128]{1,0:T(8,128)(2,1)S(1)} %copy-done.3, ...), custom_call_target="tpu_custom_call" | custom-call | tf_op jit(solution)/shard_map/pallas_call | solution.py:445
Async XLA Ops:
  0.0 277.8 %copy-start.4 = (bf16[128,128]{1,0:T(8,128)(2,1)S(1)}, bf16[128,128]{1,0:T(8,128)(2,1)}, u32[]{:S(2)}) copy-start(bf16[128,128]{1,0:T(8,128)(2,1)} %out_weight.3) | copy-start | bytes 98308
  0.0 277.8 %copy-start.3 = (bf16[128,128]{1,0:T(8,128)(2,1)S(1)}, bf16[128,128]{1,0:T(8,128)(2,1)}, u32[]{:S(2)}) copy-start(bf16[128,128]{1,0:T(8,128)(2,1)} %gate_weight.3) | copy-start | bytes 98308
  0.0 277.8 %copy-start.8 = (f32[128]{0:T(128)S(1)}, f32[128]{0:T(128)}, u32[]{:S(2)}) copy-start(f32[128]{0:T(128)} %param.18) | copy-start | bytes 1540
  0.0 277.8 %copy-start.7 = (f32[128]{0:T(128)S(1)}, f32[128]{0:T(128)}, u32[]{:S(2)}) copy-start(f32[128]{0:T(128)} %param.17) | copy-start | bytes 1540
  0.0 277.8 %copy-start.6 = (f32[128]{0:T(128)S(1)}, f32[128]{0:T(128)}, u32[]{:S(2)}) copy-start(f32[128]{0:T(128)} %param.14) | copy-start | bytes 1540
  0.0 277.8 %copy-start.5 = (f32[128]{0:T(128)S(1)}, f32[128]{0:T(128)}, u32[]{:S(2)}) copy-start(f32[128]{0:T(128)} %param.13) | copy-start | bytes 1540
  0.0 277.8 %copy-start = (bf16[1,128,128,128]{3,2,1,0:T(8,128)(2,1)S(1)}, bf16[1,128,128,128]{3,2,1,0:T(8,128)(2,1)}, u32[]{:S(2)}) copy-start(bf16[1,128,128,128]{3,2,1,0:T(8,128)(2,1)} %param.10) | copy-start | bytes 12582916
  277.8 2.2 copy-start.1
  280.0 1.0 copy-start.2

commit v4 on v3

--- a/solution.py
+++ b/solution.py
@@ -65,7 +65,9 @@
     bias_cols,
     stage,
     last,
+    held,
     sems,
+    held_sems,
 ):
     side = partial.shape[0]
     channels = out_weight.shape[0]
@@ -73,11 +75,19 @@
     copies = []
     for index in range(side // rows - 1):
         span = pl.ds(index * rows, rows)
-        copies.append(pltpu.make_async_copy(partial.at[span], update.at[span], sems.at[index]))
-        copies[-1].start()
+        copies.append(
+            (
+                pltpu.make_async_copy(partial.at[span], held.at[span], held_sems.at[index]),
+                pltpu.make_async_copy(held.at[span], update.at[span], sems.at[index]),
+            )
+        )
+        copies[-1][0].start()
     gain_cols[...] = jnp.broadcast_to(out_gain[...], (side, channels)).T
     bias_cols[...] = jnp.broadcast_to(out_bias[...], (side, channels)).T
     unpack_mixed(mixed, stage, rows)
+    for fetch, store in copies:
+        fetch.wait()
+        store.start()
 
     def finish(row, carry):
         last[row] = finish_row(
@@ -95,8 +105,8 @@
         last, update.at[pl.ds(side - rows, rows)], sems.at[side // rows - 1]
     )
     copy.start()
-    for other in copies:
-        other.wait()
+    for _, store in copies:
+        store.wait()
     copy.wait()
 
 
@@ -458,9 +468,11 @@
             pltpu.VMEM((channels, side), jnp.float32),
             pltpu.VMEM((channels * last, side), jnp.float32),
             pltpu.VMEM((last, side, width), jnp.bfloat16),
+            pltpu.VMEM((side, side, width), jnp.bfloat16),
+            pltpu.SemaphoreType.DMA((side // last,)),
             pltpu.SemaphoreType.DMA((side // last,)),
         ],
-        compiler_params=pltpu.CompilerParams(vmem_limit_bytes=32 * 1024 * 1024),
+        compiler_params=pltpu.CompilerParams(vmem_limit_bytes=60 * 1024 * 1024),
     )(
         partial,
         mixed_last,

time: 288 us -> 287 us (level)
  local copies, waits for them, and re-layouts: 3.25 us -> 0 us
  Pallas kernels: 281 us -> 284 us
    unnamed x18 -> x0, local copies, waits for them, and re-layouts: 3.25 us -> none
    pallas_call x1, Pallas kernels: 3.38 us -> 6.59 us  [shards(): pl.pallas_call(finish_kernel, grid=(1,), out_shape=jax.ShapeDtypeStruct((...]
where the time goes in v4:
time: 287 us; the launch traced here: 284 us
  Pallas kernels  284 us (99%)
    pallas_call x1, Pallas kernels, shards(): pl.pallas_call(functools.partial(kernel, n, most_tiles), out_shape=(jax.S...  277 us
    pallas_call x1, Pallas kernels, shards(): pl.pallas_call(finish_kernel, grid=(1,), out_shape=jax.ShapeDtypeStruct((...  6.59 us

profile of v4, /device:TPU:15, one launch (start us, length us, event | category | flops | bytes accessed | tf_op | source)
XLA Modules:
  0.0 283.8 jit_solution(13589330122489307422)
XLA Ops:
  0.0 277.2 %shard_map.100 = (bf16[128,128,128]{2,1,0:T(8,128)(2,1)}, bf16[16,8,16,128]{3,2,1,0:T(8,128)(2,1)}) custom-call(s32[2]{0:T(128)} %comp_len.1, s32[16]{0:T(128)} %tile_place.1, bf16[128,128,128]{2,1,0:T(8,128)(2,1)} %bitcast.6, f32[1,128]{1,0:T(1,128)} %bitcast.8, f32[1,128]{1,0:T(1,128)} %bitcast.10, bf16[128,512]{1,0:T(8,128)(2,1)} %proj_weight.1, ...), custom_call_target="tpu_custom_call" | custom-call | tf_op jit(solution)/shard_map/pallas_call | solution.py:409
  277.3 6.6 %shard_map.101 = bf16[128,128,128]{2,1,0:T(8,128)(2,1)} custom-call(bf16[128,128,128]{2,1,0:T(8,128)(2,1)} %get-tuple-element.7.partial, bf16[16,8,16,128]{3,2,1,0:T(8,128)(2,1)} %get-tuple-element.8.mixed, bf16[128,128,128]{2,1,0:T(8,128)(2,1)} %bitcast.7, f32[1,128]{1,0:T(1,128)} %bitcast.9, f32[1,128]{1,0:T(1,128)} %bitcast.11, ...), custom_call_target="tpu_custom_call" | custom-call | tf_op jit(solution)/shard_map/pallas_call | solution.py:455
